TPU v7x, 512 devices: a whole 4x4x16 slice. The times are simulated.
512 devices in a mesh: areal: 32 (over y, x, core), layer: 16 (over z).
Axes of the slice: x: 4, y: 4, z: 16, core: 2. Of those that a mesh axis runs over, the one named last changes fastest.
Arguments:
- rhs: bfloat16 [32, 32, 112, 384], P('areal', 'layer'), may hold values from -6 to 6
- areal_blocks: bfloat16 [32, 32, 6, 384, 384], P('areal', 'layer'), may hold values from -0.078125 to 0.078125
- vertical_blocks: bfloat16 [32, 32, 2, 384, 384], P('areal', 'layer'), may hold values from -0.078125 to 0.078125
- conn_src: int32 [32, 16, 6], P('areal', 'layer'), may hold values from 0 to 63, as said below
- conn_count: int32 [32, 16], P('areal', 'layer'), may hold values from 1 to 6, as said below
- tile_map: int32 [64], replicated, may hold values from 0 to 63, as said below
- well_cells: int32 [32, 32, 4], P('areal', 'layer'), may hold values from 0 to 127
- well_gain: float32 [32, 32, 4], P('areal', 'layer'), may hold values from -24 to 24
- sens: float32 [32, 32, 3, 128], P('areal', 'layer'), may hold values from -6 to 6
- basis: bfloat16 [32, 32, 128, 256], P('areal', 'layer'), may hold values from -0.015625 to 0.015625
Outputs:
- adjoint: bfloat16 [32, 32, 112, 384], P('areal', 'layer')
- coefficients: bfloat16 [112, 256], P('layer', 'areal')
Inputs may be any that keep to these rules, and one draw needn't show every extreme that they name: Tile t of a layer group's plane is held by device column tile_map[t] // 2 in tile layer 2 g + tile_map[t] % 2; each value is held by one tile. `conn_src`: the 6 sources of device column c lie, in some order, on the 6 device columns (c + k) mod 32 with k one of 1 to 2, their negatives, 16 and 17, one on each. `conn_count`: the live connections of a device are its first ones. `well_cells`: cells of a tile, repeats allowed.
All inputs are finite; a program needn't handle non-finite values.
Results may differ from a plain program's by a relative error of at most 0.02.
Values may be sent and summed in bfloat16 or wider, within the bound.
A program may use at most 64 MiB of HBM per device.

v0:
```python
import jax
import jax.numpy as jnp
from jax import lax
from jax.sharding import PartitionSpec as P

ITERS = 3


def extended(x, sides, width):
    for axis, dim in sides:
        size, length = (lax.axis_size(axis), x.shape[dim])
        up = [(i, (i + 1) % size) for i in range(size - 1)]
        down = [(j, i) for i, j in up]
        last = lax.slice_in_dim(x, length - width, length, axis=dim)
        leading = lax.slice_in_dim(x, 0, width, axis=dim)
        before = lax.ppermute(last, axis, up)
        after = lax.ppermute(leading, axis, down)
        x = jnp.concatenate([before, x, after], axis=dim)
    return x


def on_device(
    rhs,
    areal_blocks,
    vertical_blocks,
    conn_src,
    conn_count,
    tile_map,
    well_cells,
    well_gain,
    sens,
    basis,
):
    cells = sens.shape[-1]
    phases = sens.shape[-2]
    rows = rhs.shape[2]
    sources = conn_src[0, 0]
    place = jnp.take(tile_map, sources)
    peer = place // 2
    slot = place % 2
    live = jnp.arange(sources.shape[0], dtype=jnp.int32) < conn_count[0, 0]
    blocks = areal_blocks[0]
    vert_blocks = vertical_blocks[0]
    rhs_float = rhs[0].astype(jnp.float32)
    lam = rhs
    for step in range(ITERS):
        whole = lax.all_gather(lam, "areal", axis=0, tiled=True)
        chosen = whole[peer, slot]
        chosen = jnp.where(live[:, None, None], chosen, jnp.zeros_like(chosen))
        padded = extended(lam, (("layer", 1),), 1)[0]
        near = jnp.stack([padded[0:2], padded[2:4]], axis=1)
        off = jnp.einsum("sru,dsuv->drv", chosen, blocks, preferred_element_type=jnp.float32)
        off = off + jnp.einsum(
            "dkru,dkuv->drv", near, vert_blocks, preferred_element_type=jnp.float32
        )
        lam = (rhs_float - off).astype(jnp.bfloat16)[None]
    lamf = lam[0].astype(jnp.float32).reshape(2, rows, phases, cells)
    grad = jnp.sum(lamf * sens[0][:, None, :, :], axis=2)
    hits = well_cells[0][:, :, None] == jnp.arange(cells, dtype=jnp.int32)[None, None, :]
    well_sum = jnp.sum(jnp.where(hits, well_gain[0][:, :, None], 0.0), axis=1)
    grad = (grad + well_sum[:, None, :] * lamf[:, :, 0, :]).astype(jnp.bfloat16)
    partial_sum = jnp.einsum("jrc,jcm->rm", grad, basis[0], preferred_element_type=jnp.float32)
    reduced = lax.psum_scatter(partial_sum, "areal", scatter_dimension=1, tiled=True)
    reduced = lax.psum_scatter(reduced, "layer", scatter_dimension=0, tiled=True)
    return (lam, reduced.astype(jnp.bfloat16))


def solution(mesh):
    in_specs = (
        P("areal", "layer", None, None),
        P("areal", "layer", None, None, None),
        P("areal", "layer", None, None, None),
        P("areal", "layer", None),
        P("areal", "layer"),
        P(),
        P("areal", "layer", None),
        P("areal", "layer", None),
        P("areal", "layer", None, None),
        P("areal", "layer", None, None),
    )
    out_specs = (P("areal", "layer", None, None), P("layer", "areal"))
    return jax.shard_map(
        on_device, mesh=mesh, in_specs=in_specs, out_specs=out_specs, check_vma=False
    )
```

profile of v0, /device:TPU:1, one launch (start us, length us, event | category | flops | bytes accessed | tf_op | source)
XLA Modules:
  0.0 391.9 jit_solution(2308188141515170945)
XLA Ops:
  8.0 1.9 fusion.93
  9.9 5.0 %collective-permute-start = (bf16[1,1,112,384]{3,2,1,0:T(8,128)(2,1)}, bf16[1,1,112,384]{3,2,1,0:T(8,128)(2,1)}, u32[]{:S(2)}, u32[]{:S(2)}) collective-permute-start(bf16[1,1,112,384]{3,2,1,0:T(8,128)(2,1)} %get-tuple-element.20), channel_id=1, source_target_pairs={{0,1},{1,2},{2,3},{3,4},{4,5},{5,6},{6,7},{7,8},{8,9},{9,10},{10,1... | collective-permute-start | bytes 258056 | tf_op jit(solution)/shard_map/ppermute | solution.py:16
  14.9 1.3 collective-permute-start.1
  17.5 1.3 gather_fusion
  20.4 1.1 fusion.70
  21.4 2.4 convolution_bitcast_fusion.2
  23.8 56.2 %all-gather.6.cloned.1.call-done = bf16[32,2,112,384]{3,2,1,0:T(8,128)(2,1)} async-done(((bf16[1,2,112,384]{3,2,1,0:T(8,128)(2,1)}), bf16[32,2,112,384]{3,2,1,0:T(8,128)(2,1)}) %all-gather.6.cloned.1.call-update) | async-done | bytes 5505040 | tf_op jit(solution)/shard_map/all_gather | solution.py:47
  80.0 4.0 %gather_fusion.1 = bf16[6,112,384]{2,1,0:T(8,128)(2,1)} fusion(bf16[32,2,112,384]{3,2,1,0:T(8,128)(2,1)} %all-gather.6.cloned.1.call-done, s32[6]{0:T(128)S(1)} %fusion.82), kind=kCustom, calls=%fused_computation.1 | custom fusion | bytes 1032240 | tf_op jit(solution)/shard_map/gather | solution.py:48
  84.0 2.5 fusion.33
  87.6 3.2 collective-permute-start.2
  90.8 1.3 collective-permute-start.3
  92.3 3.7 collective-permute-done.3
  96.0 1.0 fusion.68
  97.0 2.4 convolution_bitcast_fusion.1
  99.4 49.9 %all-gather.8.cloned.1.call-done = bf16[64,112,384]{2,1,0:T(8,128)(2,1)} async-done(((bf16[2,112,384]{2,1,0:T(8,128)(2,1)}), bf16[64,112,384]{2,1,0:T(8,128)(2,1)}) %all-gather.8.cloned.1.call-update) | async-done | bytes 5505040 | tf_op jit(solution)/shard_map/all_gather | solution.py:47
  149.3 4.0 %gather_fusion.2 = bf16[6,112,384]{2,1,0:T(8,128)(2,1)} fusion(bf16[32,2,112,384]{3,2,1,0:T(8,128)(2,1)} %bitcast.157, s32[6]{0:T(128)S(1)} %fusion.82), kind=kCustom, calls=%fused_computation.2 | custom fusion | bytes 1032240 | tf_op jit(solution)/shard_map/gather | solution.py:48
  153.3 2.5 fusion.36
  156.9 3.2 collective-permute-start.4
  160.1 1.3 collective-permute-start.5
  162.2 3.1 collective-permute-done.5
  165.3 1.0 fusion.66
  166.3 2.4 convolution_bitcast_fusion
  168.7 49.9 %all-gather.10.cloned.1.call-done = bf16[64,112,384]{2,1,0:T(8,128)(2,1)} async-done(((bf16[2,112,384]{2,1,0:T(8,128)(2,1)}), bf16[64,112,384]{2,1,0:T(8,128)(2,1)}) %all-gather.10.cloned.1.call-update) | async-done | bytes 5505040 | tf_op jit(solution)/shard_map/all_gather | solution.py:47
  218.5 4.0 %gather_fusion.3 = bf16[6,112,384]{2,1,0:T(8,128)(2,1)} fusion(bf16[32,2,112,384]{3,2,1,0:T(8,128)(2,1)} %bitcast.156, s32[6]{0:T(128)S(1)} %fusion.82), kind=kCustom, calls=%fused_computation.3 | custom fusion | bytes 1032240 | tf_op jit(solution)/shard_map/gather | solution.py:48
  222.6 2.5 fusion.39
  225.1 1.8 copy.34
  226.9 1.2 multiply_reduce_fusion
  228.1 1.9 convolution_bitcast_fusion.3
  230.0 1.3 dynamic-slice.2
  231.3 1.3 dynamic-slice
  233.9 125.7 %all-reduce.4.cloned.1.call-done = f32[112,256]{0,1:T(8,128)} async-done(((f32[112,256]{0,1:T(8,128)}), f32[112,256]{0,1:T(8,128)}) %all-reduce.4.cloned.1.call-update) | async-done | bytes 114704
  360.3 24.3 %all-reduce.1 = bf16[112,8]{0,1:T(8,128)(2,1)S(1)} all-reduce(f32[112,8]{0,1:T(8,128)S(1)} %constant_dynamic-slice_fusion), channel_id=5, replica_groups=mesh['areal'=32,'layer'=16] {'layer'}, use_global_device_ids=true, to_apply=%region_3.4.clone | all-reduce | flops 896 | bytes 5376
  (27 shorter events, 7.5 us)
Async XLA Ops:
  7.2 76.9 %copy-start = (bf16[1,2,6,384,384]{4,3,2,1,0:T(8,128)(2,1)S(1)}, bf16[1,2,6,384,384]{4,3,2,1,0:T(8,128)(2,1)}, u32[]{:S(2)}) copy-start(bf16[1,2,6,384,384]{4,3,2,1,0:T(8,128)(2,1)} %param.11) | copy-start | bytes 10616836
  7.2 72.9 %all-gather.6.cloned.1.call-start = ((), (), s32[]{:S(2)}) async-start(), calls=%async_computation | async-start | bytes 5677056 | tf_op jit(solution)/shard_map/all_gather | solution.py:47
  7.9 141.4 %all-gather.8.cloned.1.call-start = ((), (), s32[]{:S(2)}) async-start(), calls=%async_computation.1 | async-start | bytes 5677056 | tf_op jit(solution)/shard_map/all_gather | solution.py:47
  9.9 9.6 %collective-permute-start = (bf16[1,1,112,384]{3,2,1,0:T(8,128)(2,1)}, bf16[1,1,112,384]{3,2,1,0:T(8,128)(2,1)}, u32[]{:S(2)}, u32[]{:S(2)}) collective-permute-start(bf16[1,1,112,384]{3,2,1,0:T(8,128)(2,1)} %get-tuple-element.20), channel_id=1, source_target_pairs={{0,1},{1,2},{2,3},{3,4},{4,5},{5,6},{6,7},{7,8},{8,9},{9,10},{10,1... | collective-permute-start | bytes 258056 | tf_op jit(solution)/shard_map/ppermute | solution.py:16
  14.9 5.5 %collective-permute-start.1 = (bf16[1,1,112,384]{3,2,1,0:T(8,128)(2,1)}, bf16[1,1,112,384]{3,2,1,0:T(8,128)(2,1)}, u32[]{:S(2)}, u32[]{:S(2)}) collective-permute-start(bf16[1,1,112,384]{3,2,1,0:T(8,128)(2,1)} %get-tuple-element.21), channel_id=1, source_target_pairs={{1,0},{2,1},{3,2},{4,3},{5,4},{6,5},{7,6},{8,7},{9,8},{10,9},{11,1... | collective-permute-start | bytes 258056 | tf_op jit(solution)/shard_map/ppermute | solution.py:17
  86.6 131.9 %all-gather.10.cloned.1.call-start = ((), (), s32[]{:S(2)}) async-start(), calls=%async_computation.2 | async-start | bytes 5677056 | tf_op jit(solution)/shard_map/all_gather | solution.py:47
  87.6 4.7 %collective-permute-start.2 = (bf16[1,1,112,384]{3,2,1,0:T(8,128)(2,1)S(1)}, bf16[1,1,112,384]{3,2,1,0:T(8,128)(2,1)S(1)}, u32[]{:S(2)}, u32[]{:S(2)}) collective-permute-start(bf16[1,1,112,384]{3,2,1,0:T(8,128)(2,1)S(1)} %get-tuple-element.16), channel_id=1, source_target_pairs={{0,1},{1,2},{2,3},{3,4},{4,5},{5,6},{6,7},{7,8},{8,9},{9,10},{10,1... | collective-permute-start | bytes 258056 | tf_op jit(solution)/shard_map/ppermute | solution.py:16
  90.8 5.2 %collective-permute-start.3 = (bf16[1,1,112,384]{3,2,1,0:T(8,128)(2,1)S(1)}, bf16[1,1,112,384]{3,2,1,0:T(8,128)(2,1)S(1)}, u32[]{:S(2)}, u32[]{:S(2)}) collective-permute-start(bf16[1,1,112,384]{3,2,1,0:T(8,128)(2,1)S(1)} %get-tuple-element.17), channel_id=1, source_target_pairs={{1,0},{2,1},{3,2},{4,3},{5,4},{6,5},{7,6},{8,7},{9,8},{10,9},{11,1... | collective-permute-start | bytes 258056 | tf_op jit(solution)/shard_map/ppermute | solution.py:17
  97.0 58.9 %copy-start.1 = (f32[1,2,3,128]{3,1,2,0:T(2,128)S(1)}, f32[1,2,3,128]{3,1,2,0:T(2,128)}, u32[]{:S(2)}) copy-start(f32[1,2,3,128]{3,1,2,0:T(2,128)} %param.18) | copy-start | bytes 9220
  155.9 203.7 %all-reduce.4.cloned.1.call-start = ((), (), s32[]{:S(2)}) async-start(), calls=%async_computation.3 | async-start | bytes 262144
  156.9 5.3 %collective-permute-start.4 = (bf16[1,1,112,384]{3,2,1,0:T(8,128)(2,1)S(1)}, bf16[1,1,112,384]{3,2,1,0:T(8,128)(2,1)S(1)}, u32[]{:S(2)}, u32[]{:S(2)}) collective-permute-start(bf16[1,1,112,384]{3,2,1,0:T(8,128)(2,1)S(1)} %get-tuple-element.12), channel_id=1, source_target_pairs={{0,1},{1,2},{2,3},{3,4},{4,5},{5,6},{6,7},{7,8},{8,9},{9,10},{10,1... | collective-permute-start | bytes 258056 | tf_op jit(solution)/shard_map/ppermute | solution.py:16
  160.1 5.2 %collective-permute-start.5 = (bf16[1,1,112,384]{3,2,1,0:T(8,128)(2,1)S(1)}, bf16[1,1,112,384]{3,2,1,0:T(8,128)(2,1)S(1)}, u32[]{:S(2)}, u32[]{:S(2)}) collective-permute-start(bf16[1,1,112,384]{3,2,1,0:T(8,128)(2,1)S(1)} %get-tuple-element.13), channel_id=1, source_target_pairs={{1,0},{2,1},{3,2},{4,3},{5,4},{6,5},{7,6},{8,7},{9,8},{10,9},{11,1... | collective-permute-start | bytes 258056 | tf_op jit(solution)/shard_map/ppermute | solution.py:17
Sparse Core Ops, SparseCore 0:
  11.1 68.8 all-gather.5
  86.7 62.5 all-gather.7
  156.0 62.5 all-gather.9
  230.1 129.4 all-reduce.3
where the time goes:
time: 400 us; the launch traced here: 392 us
  waiting for transfers between devices  290 us (72%)
  blocking collectives  24.3 us (6%)
  local copies, waits for them, and re-layouts  22.9 us (6%)
  matrix products  16.6 us (4%)
  between operations  15.8 us (4%)
  starting transfers between devices  15.4 us (4%)
  other arithmetic  6.32 us (2%)
    all_gather x3, waiting for transfers between devices, on_device(): whole = lax.all_gather(lam, 'areal', axis=0, tiled=True)  156 us
    unnamed x5, waiting for transfers between devices  126 us
    unnamed x1, blocking collectives  24.3 us
    gather x3, local copies, waits for them, and re-layouts, on_device(): chosen = whole[peer, slot]  12 us
    ppermute x3, starting transfers between devices, extended(): before = lax.ppermute(last, axis, up)  11.4 us
  transfers between devices with their start and end apart: 10, of which 8 were waited for; matrix products, arithmetic and copies ran while one was open for 5% of the time, Pallas kernels for 0%

commit v1 on v0

v1 whole, which is shorter than its diff:
```python
import jax
import jax.numpy as jnp
from jax import lax
from jax.experimental import pallas as pl
from jax.experimental.pallas import tpu as pltpu
from jax.sharding import PartitionSpec as P

ITERS = 3
COLUMNS = 32
GROUPS = 16
ROWS = 112
U = 384
CELLS = 128
MODES = 256
NS = 6
WELLS = 4
PER = ROWS // GROUPS
OFFSETS = (1, 2, -1, -2, 16, 17)
ORDER = (5, 4, 0, 1, 2, 3)
CHUNKS = ((0, 64), (64, 48))
MESH = pl.DeviceIdType.MESH
F32, BF16, I32 = jnp.float32, jnp.bfloat16, jnp.int32


def kernel(
    conn_src,
    conn_count,
    tile_map,
    well_cells,
    well_gain,
    rhs_hbm,
    areal_hbm,
    vert_hbm,
    sens_hbm,
    basis_hbm,
    adjoint_hbm,
    coef_ref,
    lam,
    w,
    v,
    sens,
    basis,
    send,
    recvz,
    req_out,
    req_in,
    part,
    part_in,
    scat,
    scat_in,
    adj,
    *rest,
):
    recv = [[rest[i * len(CHUNKS) + h] for h in range(len(CHUNKS))] for i in range(ITERS)]
    (
        load_sem,
        out_sem,
        req_ss,
        req_rs,
        a_ss,
        a_rs,
        z_ss,
        z_rs,
        p_ss,
        p_rs,
        s_ss,
        s_rs,
    ) = rest[ITERS * len(CHUNKS) :]
    c, g = lax.axis_index("areal"), lax.axis_index("layer")

    loads = [
        pltpu.make_async_copy(rhs_hbm.at[0], lam.at[0, pl.ds(0, 2)], load_sem.at[0]),
        pltpu.make_async_copy(vert_hbm.at[0], v, load_sem.at[1]),
        pltpu.make_async_copy(areal_hbm.at[0], w, load_sem.at[2]),
        pltpu.make_async_copy(sens_hbm.at[0], sens, load_sem.at[3]),
        pltpu.make_async_copy(basis_hbm.at[0], basis, load_sem.at[4]),
    ]
    for one in loads:
        one.start()

    barrier = pltpu.get_barrier_semaphore()
    for k in range(1, COLUMNS):
        pl.semaphore_signal(barrier, inc=1, device_id=(lax.rem(c + k, COLUMNS), g), device_id_type=MESH)
    for k in range(1, GROUPS):
        pl.semaphore_signal(barrier, inc=1, device_id=(c, lax.rem(g + k, GROUPS)), device_id_type=MESH)

    count = conn_count[0, 0]
    where, wanted = [], []
    for s in range(NS):
        place = tile_map[conn_src[0, 0, s]]
        delta = lax.rem((place >> 1) - c + COLUMNS, COLUMNS)
        at = I32(0)
        for k, offset in enumerate(OFFSETS):
            at = jnp.where(delta == offset % COLUMNS, I32(k), at)
        where.append(at)
        wanted.append(jnp.where(s < count, place & 1, I32(2)))
    for k in range(NS):
        ask = I32(2)
        for s in range(NS):
            ask = jnp.where(where[s] == k, wanted[s], ask)
        req_out[k] = jnp.full((8, 128), ask, I32)
    part[...] = jnp.zeros((COLUMNS, 8, 128), F32)
    for i in range(ITERS):
        lam[i, 2] = jnp.zeros((ROWS, U), BF16)

    pl.semaphore_wait(barrier, COLUMNS + GROUPS - 2)

    asks = []
    for k in ORDER:
        one = pltpu.make_async_remote_copy(
            req_out.at[k], req_in.at[k], req_ss.at[k], req_rs.at[k],
            device_id=(lax.rem(c + OFFSETS[k] + COLUMNS, COLUMNS), g), device_id_type=MESH,
        )
        one.start()
        asks.append(one)

    up, down = lax.rem(g + 1, GROUPS), lax.rem(g + GROUPS - 1, GROUPS)

    def send_vertical(i, h):
        first, rows = CHUNKS[h]
        at = pl.ds(first, rows)
        out = []
        for side, to in ((0, up), (1, down)):
            one = pltpu.make_async_remote_copy(
                lam.at[i, 1 - side, at], recvz.at[i, side, at], z_ss.at[i, h, side], z_rs.at[i, h, side],
                device_id=(c, to), device_id_type=MESH,
            )
            one.start()
            out.append(one)
        return out

    def send_areal(i, h, slots):
        first, rows = CHUNKS[h]
        at = pl.ds(first, rows)
        out = []
        for k in ORDER:
            send[i, k, at] = lam[i, slots[k], at]
            one = pltpu.make_async_remote_copy(
                send.at[i, k, at], recv[i][h].at[k], a_ss.at[i, h, k], a_rs.at[i, h, k],
                device_id=(lax.rem(c - OFFSETS[k] + COLUMNS, COLUMNS), g), device_id_type=MESH,
            )
            one.start()
            out.append(one)
        return out

    flying = {}
    loads[0].wait()
    for h in range(len(CHUNKS)):
        flying[0, h] = send_vertical(0, h)
    for one in asks:
        one.wait_recv()
    slots = [jnp.max(req_in[k]) for k in range(NS)]
    for h in range(len(CHUNKS)):
        flying[0, h] = flying[0, h] + send_areal(0, h, slots)

    for one in loads[1:]:
        one.wait()

    cell = lax.broadcasted_iota(I32, (1, CELLS), 1)
    weight = []
    for d in range(2):
        wells = jnp.zeros((1, CELLS), F32)
        for k in range(WELLS):
            wells += jnp.where(cell == well_cells[0, d, k], well_gain[0, d, k], 0.0)
        weight.append([sens[d, 0:1] + wells, sens[d, 1:2], sens[d, 2:3]])

    stored = []
    for i in range(ITERS):
        for h, (first, rows) in enumerate(CHUNKS):
            at = pl.ds(first, rows)
            for one in flying[i, h]:
                one.wait_recv()
            below = jnp.where(g > 0, recvz[i, 0, at], jnp.zeros((rows, U), BF16))
            above = jnp.where(g < GROUPS - 1, recvz[i, 1, at], jnp.zeros((rows, U), BF16))
            sides = ((below, lam[i, 1, at]), (lam[i, 0, at], above))
            chosen = jnp.concatenate([recv[i][h][where[s]] for s in range(NS)], axis=1)
            grads = []
            for d in range(2):
                off = jnp.dot(chosen, w[d].reshape(NS * U, U), preferred_element_type=F32)
                near = jnp.concatenate(sides[d], axis=1)
                off += jnp.dot(near, v[d].reshape(2 * U, U), preferred_element_type=F32)
                new = (lam[0, d, at].astype(F32) - off).astype(BF16)
                if i < ITERS - 1:
                    lam[i + 1, d, at] = new
                else:
                    adj[d, at] = new
                    newf = new.astype(F32)
                    grad = newf[:, :CELLS] * weight[d][0]
                    for p in range(1, 3):
                        grad += newf[:, p * CELLS : (p + 1) * CELLS] * weight[d][p]
                    grads.append(grad.astype(BF16))
            if i < ITERS - 1:
                flying[i + 1, h] = send_areal(i + 1, h, slots) + send_vertical(i + 1, h)
            else:
                grad = jnp.concatenate(grads, axis=1)
                scat_rows = jnp.dot(grad, basis[...].reshape(2 * CELLS, MODES), preferred_element_type=F32)
                part[:, :, first : first + rows] = scat_rows.T.reshape(COLUMNS, 8, rows)

    store = pltpu.make_async_copy(adj, adjoint_hbm.at[0], out_sem)
    store.start()

    parts = []
    for k in range(1, COLUMNS):
        to = lax.rem(c + k, COLUMNS)
        one = pltpu.make_async_remote_copy(
            part.at[to], part_in.at[k], p_ss.at[k], p_rs.at[k], device_id=(to, g), device_id_type=MESH
        )
        one.start()
        parts.append(one)

    big = lax.broadcasted_iota(I32, (8 * 128, 128), 0)
    lane = lax.broadcasted_iota(I32, (8 * 128, 128), 1)
    row = big & 127
    pick = jnp.where((row < ROWS) & (lane == 8 * lax.rem(row, PER) + (big >> 7)), 1.0, 0.0).astype(BF16)
    group = lax.broadcasted_iota(I32, (GROUPS, 128), 0)
    held = lax.broadcasted_iota(I32, (GROUPS, 128), 1)
    mine = (held >= PER * group) & (held < PER * group + PER)

    total = part[c]
    for one in parts:
        one.wait_recv()
    for k in range(1, COLUMNS):
        total += part_in[k]
    spread = jnp.concatenate(
        [jnp.where(mine, jnp.broadcast_to(total[m : m + 1], (GROUPS, 128)), 0.0).astype(BF16) for m in range(8)],
        axis=1,
    )
    packed = jnp.dot(spread, pick, preferred_element_type=F32)
    scat[...] = packed.reshape(GROUPS, 1, 128)

    scats = []
    for k in range(1, GROUPS):
        to = lax.rem(g + k, GROUPS)
        one = pltpu.make_async_remote_copy(
            scat.at[to], scat_in.at[k], s_ss.at[k], s_rs.at[k], device_id=(c, to), device_id_type=MESH
        )
        one.start()
        scats.append(one)
    line = scat[g]
    for one in scats:
        one.wait_recv()
    for k in range(1, GROUPS):
        line += scat_in[k]
    sub = lax.broadcasted_iota(I32, (8, 128), 0)
    lane8 = lax.broadcasted_iota(I32, (8, 128), 1)
    rows8 = jnp.where((lane8 >> 3) == sub, jnp.broadcast_to(line, (8, 128)), 0.0).astype(BF16)
    l128 = lax.broadcasted_iota(I32, (128, 128), 0)
    m128 = lax.broadcasted_iota(I32, (128, 128), 1)
    fold = jnp.where((l128 & 7) == m128, 1.0, 0.0).astype(BF16)
    result = jnp.dot(rows8, fold, preferred_element_type=F32).astype(BF16)
    coef_ref[...] = result[:PER, :8]

    for one in asks + parts + scats:
        one.wait_send()
    for i in range(ITERS):
        for h in range(len(CHUNKS)):
            for one in flying[i, h]:
                one.wait_send()
    store.wait()


def on_device(rhs, areal_blocks, vertical_blocks, conn_src, conn_count, tile_map, well_cells, well_gain, sens, basis):
    smem = pl.BlockSpec(memory_space=pltpu.SMEM)
    hbm = pl.BlockSpec(memory_space=pl.ANY)
    nc = len(CHUNKS)
    dma = pltpu.SemaphoreType.DMA
    return pl.pallas_call(
        kernel,
        out_shape=(
            jax.ShapeDtypeStruct((1, 2, ROWS, U), BF16),
            jax.ShapeDtypeStruct((PER, MODES // COLUMNS), BF16),
        ),
        in_specs=[smem] * 5 + [hbm] * 5,
        out_specs=(hbm, pl.BlockSpec(memory_space=pltpu.VMEM)),
        scratch_shapes=[
            pltpu.VMEM((ITERS, 3, ROWS, U), BF16),
            pltpu.VMEM((2, NS, U, U), BF16),
            pltpu.VMEM((2, 2, U, U), BF16),
            pltpu.VMEM((2, 3, CELLS), F32),
            pltpu.VMEM((2, CELLS, MODES), BF16),
            pltpu.VMEM((ITERS, NS, ROWS, U), BF16),
            pltpu.VMEM((ITERS, 2, ROWS, U), BF16),
            pltpu.VMEM((NS, 8, 128), I32),
            pltpu.VMEM((NS, 8, 128), I32),
            pltpu.VMEM((COLUMNS, 8, 128), F32),
            pltpu.VMEM((COLUMNS, 8, 128), F32),
            pltpu.VMEM((GROUPS, 1, 128), F32),
            pltpu.VMEM((GROUPS, 1, 128), F32),
            pltpu.VMEM((2, ROWS, U), BF16),
        ]
        + [pltpu.VMEM((NS, rows, U), BF16) for _ in range(ITERS) for _, rows in CHUNKS]
        + [
            dma((5,)),
            dma,
            dma((NS,)),
            dma((NS,)),
            dma((ITERS, nc, NS)),
            dma((ITERS, nc, NS)),
            dma((ITERS, nc, 2)),
            dma((ITERS, nc, 2)),
            dma((COLUMNS,)),
            dma((COLUMNS,)),
            dma((GROUPS,)),
            dma((GROUPS,)),
        ],
        compiler_params=pltpu.CompilerParams(
            collective_id=0, has_side_effects=True, vmem_limit_bytes=56 * 1024 * 1024
        ),
        name="sweeps",
    )(conn_src, conn_count, tile_map, well_cells, well_gain, rhs, areal_blocks, vertical_blocks, sens, basis)


def solution(mesh):
    in_specs = (
        P("areal", "layer", None, None),
        P("areal", "layer", None, None, None),
        P("areal", "layer", None, None, None),
        P("areal", "layer", None),
        P("areal", "layer"),
        P(),
        P("areal", "layer", None),
        P("areal", "layer", None),
        P("areal", "layer", None, None),
        P("areal", "layer", None, None),
    )
    out_specs = (P("areal", "layer", None, None), P("layer", "areal"))
    return jax.shard_map(on_device, mesh=mesh, in_specs=in_specs, out_specs=out_specs, check_vma=False)
```

time: 400 us -> 68.2 us (0.17); the launches traced: 392 us -> 68 us
  waiting for transfers between devices: 290 us -> 0 us
  Pallas kernels: 0 us -> 62.6 us
  blocking collectives: 24.3 us -> 0 us
  local copies, waits for them, and re-layouts: 22.9 us -> 4.13 us
  matrix products: 16.6 us -> 0 us
  starting transfers between devices: 15.4 us -> 0 us
  between operations: 15.8 us -> 1.29 us
  other arithmetic: 6.32 us -> 0 us
    all_gather x3 -> x0, waiting for transfers between devices: 156 us -> none  [on_device(): whole = lax.all_gather(lam, 'areal', axis=0, tiled=True)]
    unnamed x5 -> x0, waiting for transfers between devices: 126 us -> none
    pallas_call x0 -> x1, Pallas kernels: none -> 62.6 us  [on_device(): pl.pallas_call(kernel, out_shape=(jax.ShapeDtypeStruct((1, 2, ROWS, U), B...]
    unnamed x1 -> x0, blocking collectives: 24.3 us -> none
    dot_general x7 -> x0, matrix products: 16.6 us -> none  [the longest x3 7.64 us: on_device(): jnp.einsum('sru,dsuv->drv', chosen, blocks, preferred_element_type=jnp.fl...]
    ppermute x6 -> x0, starting transfers between devices: 15.2 us -> none  [the longest x3 11.4 us: extended(): before = lax.ppermute(last, axis, up)]
    gather x4 -> x0, local copies, waits for them, and re-layouts: 13.3 us -> none  [the longest x3 12 us: on_device(): chosen = whole[peer, slot]]
    ppermute x6 -> x0, waiting for transfers between devices: 8.01 us -> none  [the longest x3 7.8 us: extended(): after = lax.ppermute(leading, axis, down)]
  transfers between devices with their start and end apart: 10 -> 0, of which waited for: 8 -> 0; matrix products, arithmetic and copies ran while one was open for 5% -> 0% of each run, Pallas kernels for 0% -> 0%
where the time goes in v1:
time: 68.2 us; the launch traced here: 68 us
  Pallas kernels  62.6 us (92%)
  local copies, waits for them, and re-layouts  4.13 us (6%)
  between operations  1.29 us (2%)
    pallas_call x1, Pallas kernels, on_device(): pl.pallas_call(kernel, out_shape=(jax.ShapeDtypeStruct((1, 2, ROWS, U), B...  62.6 us
    unnamed x3, local copies, waits for them, and re-layouts  4.13 us

profile of v1, /device:TPU:1, one launch (start us, length us, event | category | flops | bytes accessed | tf_op | source)
XLA Modules:
  0.0 68.0 jit_solution(6140964926661391911)
XLA Ops:
  1.3 1.3 %copy.12.sens_hbm = f32[1,2,3,128]{3,2,1,0:T(4,128)} copy(f32[1,2,3,128]{3,1,2,0:T(2,128)} %param.18) | data formatting | bytes 6144 | tf_op args[8]
  2.6 62.6 %sweeps.1 = (bf16[1,2,112,384]{3,2,1,0:T(8,128)(2,1)}, bf16[7,8]{1,0:T(8,128)(2,1)}) custom-call(s32[1,1,6]{2,1,0:T(1,128)} %conn_src.1, s32[1,1]{1,0:T(1,128)S(6)} %copy.15.conn_count, s32[64]{0:T(128)} %tile_map.1, s32[1,2,4]{2,1,0:T(2,128)} %well_cells.1, f32[1,2,4]{2,1,0:T(2,128)} %well_gain.1, bf16[1,2,112,384]{3,2,1,0:T(8,128)(2,1)} %rhs_hbm.1, ...), custom_call_target="tpu_custom_call" | custom-call | tf_op jit(solution)/shard_map/sweeps/pallas_call | solution.py:267
  65.2 1.6 %copy.16 = bf16[1,2,112,384]{3,2,1,0:T(8,128)(2,1)} copy(bf16[1,2,112,384]{3,2,1,0:T(8,128)(2,1)} %get-tuple-element.4) | data formatting | bytes 344064
  66.8 1.2 %copy.17 = bf16[7,8]{1,0:T(8,128)(2,1)} copy(bf16[7,8]{1,0:T(8,128)(2,1)} %get-tuple-element.5) | data formatting | bytes 224

commit v2 on v1

--- a/solution.py
+++ b/solution.py
@@ -129,11 +129,11 @@
             out.append(one)
         return out
 
-    def send_areal(i, h, slots):
+    def send_areal(i, h, slots, which=ORDER):
         first, rows = CHUNKS[h]
         at = pl.ds(first, rows)
         out = []
-        for k in ORDER:
+        for k in which:
             send[i, k, at] = lam[i, slots[k], at]
             one = pltpu.make_async_remote_copy(
                 send.at[i, k, at], recv[i][h].at[k], a_ss.at[i, h, k], a_rs.at[i, h, k],
@@ -147,11 +147,12 @@
     loads[0].wait()
     for h in range(len(CHUNKS)):
         flying[0, h] = send_vertical(0, h)
-    for one in asks:
+    slots = [None] * NS
+    for k, one in sorted(zip(ORDER, asks), key=lambda pair: pair[0]):
         one.wait_recv()
-    slots = [jnp.max(req_in[k]) for k in range(NS)]
-    for h in range(len(CHUNKS)):
-        flying[0, h] = flying[0, h] + send_areal(0, h, slots)
+        slots[k] = jnp.max(req_in[k])
+        for h in range(len(CHUNKS)):
+            flying[0, h] = flying[0, h] + send_areal(0, h, slots, (k,))
 
     for one in loads[1:]:
         one.wait()
@@ -162,7 +163,7 @@
         wells = jnp.zeros((1, CELLS), F32)
         for k in range(WELLS):
             wells += jnp.where(cell == well_cells[0, d, k], well_gain[0, d, k], 0.0)
-        weight.append([sens[d, 0:1] + wells, sens[d, 1:2], sens[d, 2:3]])
+        weight.append([sens[0, d : d + 1] + wells, sens[1, d : d + 1], sens[2, d : d + 1]])
 
     stored = []
     for i in range(ITERS):
@@ -259,12 +260,17 @@
     store.wait()
 
 
+def hand_over(adj, coef, adjoint_ref, coef_ref):
+    adjoint_ref[...] = adj[...]
+    coef_ref[...] = coef[...]
+
+
 def on_device(rhs, areal_blocks, vertical_blocks, conn_src, conn_count, tile_map, well_cells, well_gain, sens, basis):
     smem = pl.BlockSpec(memory_space=pltpu.SMEM)
     hbm = pl.BlockSpec(memory_space=pl.ANY)
     nc = len(CHUNKS)
     dma = pltpu.SemaphoreType.DMA
-    return pl.pallas_call(
+    adj, coef = pl.pallas_call(
         kernel,
         out_shape=(
             jax.ShapeDtypeStruct((1, 2, ROWS, U), BF16),
@@ -276,7 +282,7 @@
             pltpu.VMEM((ITERS, 3, ROWS, U), BF16),
             pltpu.VMEM((2, NS, U, U), BF16),
             pltpu.VMEM((2, 2, U, U), BF16),
-            pltpu.VMEM((2, 3, CELLS), F32),
+            pltpu.VMEM((3, 2, CELLS), F32),
             pltpu.VMEM((2, CELLS, MODES), BF16),
             pltpu.VMEM((ITERS, NS, ROWS, U), BF16),
             pltpu.VMEM((ITERS, 2, ROWS, U), BF16),
@@ -307,7 +313,18 @@
             collective_id=0, has_side_effects=True, vmem_limit_bytes=56 * 1024 * 1024
         ),
         name="sweeps",
-    )(conn_src, conn_count, tile_map, well_cells, well_gain, rhs, areal_blocks, vertical_blocks, sens, basis)
+    )(conn_src, conn_count, tile_map, well_cells, well_gain, rhs, areal_blocks, vertical_blocks, jnp.transpose(sens, (0, 2, 1, 3)), basis)
+    vmem = pl.BlockSpec(memory_space=pltpu.VMEM)
+    return pl.pallas_call(
+        hand_over,
+        out_shape=(
+            jax.ShapeDtypeStruct((1, 2, ROWS, U), BF16),
+            jax.ShapeDtypeStruct((PER, MODES // COLUMNS), BF16),
+        ),
+        in_specs=[vmem, vmem],
+        out_specs=(vmem, vmem),
+        name="hand_over",
+    )(adj, coef)
 
 
 def solution(mesh):

time: 68.2 us -> 66 us (0.968)
  local copies, waits for them, and re-layouts: 4.13 us -> 0 us
  Pallas kernels: 62.6 us -> 64.6 us
    unnamed x3 -> x0, local copies, waits for them, and re-layouts: 4.13 us -> none
    pallas_call x0 -> x1, Pallas kernels: none -> 1.61 us  [on_device(): pl.pallas_call(hand_over, out_shape=(jax.ShapeDtypeStruct((1, 2, ROWS, U)...]
where the time goes in v2:
time: 66 us; the launch traced here: 65.9 us
  Pallas kernels  64.6 us (98%)
  between operations  1.29 us (2%)
    pallas_call x1, Pallas kernels, on_device(): pl.pallas_call(kernel, out_shape=(jax.ShapeDtypeStruct((1, 2, ROWS, U), B...  63 us
    pallas_call x1, Pallas kernels, on_device(): pl.pallas_call(hand_over, out_shape=(jax.ShapeDtypeStruct((1, 2, ROWS, U)...  1.61 us

profile of v2, /device:TPU:1, one launch (start us, length us, event | category | flops | bytes accessed | tf_op | source)
XLA Modules:
  0.0 65.9 jit_solution(12702658966346292782)
XLA Ops:
  1.3 63.0 %sweeps.1 = (bf16[1,2,112,384]{3,2,1,0:T(8,128)(2,1)}, bf16[7,8]{1,0:T(8,128)(2,1)}) custom-call(s32[1,1,6]{2,1,0:T(1,128)} %conn_src.1, s32[1,1]{1,0:T(1,128)S(6)} %copy.12.conn_count, s32[64]{0:T(128)} %tile_map.1, s32[1,2,4]{2,1,0:T(2,128)} %well_cells.1, f32[1,2,4]{2,1,0:T(2,128)} %well_gain.1, bf16[1,2,112,384]{3,2,1,0:T(8,128)(2,1)} %rhs_hbm.1, ...), custom_call_target="tpu_custom_call" | custom-call | tf_op jit(solution)/shard_map/sweeps/pallas_call | solution.py:273
  64.3 1.6 %hand_over.1 = (bf16[1,2,112,384]{3,2,1,0:T(8,128)(2,1)}, bf16[7,8]{1,0:T(8,128)(2,1)}) custom-call(bf16[1,2,112,384]{3,2,1,0:T(8,128)(2,1)} %get-tuple-element.4.adj, bf16[7,8]{1,0:T(8,128)(2,1)} %get-tuple-element.5.coef), custom_call_target="tpu_custom_call" | custom-call | tf_op jit(solution)/shard_map/hand_over/pallas_call | solution.py:318

commit v3 on v2

--- a/solution.py
+++ b/solution.py
@@ -49,6 +49,7 @@
     scat,
     scat_in,
     adj,
+    slot_ref,
     *rest,
 ):
     recv = [[rest[i * len(CHUNKS) + h] for h in range(len(CHUNKS))] for i in range(ITERS)]
@@ -129,30 +130,44 @@
             out.append(one)
         return out
 
-    def send_areal(i, h, slots, which=ORDER):
+    def tile_copy(i, h, k):
+        first, rows = CHUNKS[h]
+        return pltpu.make_async_remote_copy(
+            send.at[i, k, pl.ds(first, rows)], recv[i][h].at[k], a_ss.at[i, h, k], a_rs.at[i, h, k],
+            device_id=(lax.rem(c - OFFSETS[k] + COLUMNS, COLUMNS), g), device_id_type=MESH,
+        )
+
+    def send_tile(i, h, k, slot):
         first, rows = CHUNKS[h]
         at = pl.ds(first, rows)
-        out = []
-        for k in which:
-            send[i, k, at] = lam[i, slots[k], at]
-            one = pltpu.make_async_remote_copy(
-                send.at[i, k, at], recv[i][h].at[k], a_ss.at[i, h, k], a_rs.at[i, h, k],
-                device_id=(lax.rem(c - OFFSETS[k] + COLUMNS, COLUMNS), g), device_id_type=MESH,
-            )
-            one.start()
-            out.append(one)
-        return out
+        send[i, k, at] = lam[i, slot, at]
+        tile_copy(i, h, k).start()
+
+    def send_areal(i, h, slots):
+        for k in ORDER:
+            send_tile(i, h, k, slots[k])
+        return [tile_copy(i, h, k) for k in range(NS)]
 
     flying = {}
     loads[0].wait()
     for h in range(len(CHUNKS)):
         flying[0, h] = send_vertical(0, h)
-    slots = [None] * NS
-    for k, one in sorted(zip(ORDER, asks), key=lambda pair: pair[0]):
-        one.wait_recv()
-        slots[k] = jnp.max(req_in[k])
-        for h in range(len(CHUNKS)):
-            flying[0, h] = flying[0, h] + send_areal(0, h, slots, (k,))
+    ask_of = dict(zip(ORDER, asks))
+
+    def serve(order):
+        for k in order:
+            ask_of[k].wait_recv()
+            slot = jnp.max(req_in[k])
+            slot_ref[k] = slot
+            for h in range(len(CHUNKS)):
+                send_tile(0, h, k, slot)
+
+    last = lax.rem(c, 8) >= 6
+    pl.when(last)(lambda: serve((0, 1, 4, 5, 2, 3)))
+    pl.when(jnp.logical_not(last))(lambda: serve((2, 3, 4, 5, 0, 1)))
+    slots = [slot_ref[k] for k in range(NS)]
+    for h in range(len(CHUNKS)):
+        flying[0, h] = flying[0, h] + [tile_copy(0, h, k) for k in range(NS)]
 
     for one in loads[1:]:
         one.wait()
@@ -293,6 +308,7 @@
             pltpu.VMEM((GROUPS, 1, 128), F32),
             pltpu.VMEM((GROUPS, 1, 128), F32),
             pltpu.VMEM((2, ROWS, U), BF16),
+            pltpu.SMEM((NS,), I32),
         ]
         + [pltpu.VMEM((NS, rows, U), BF16) for _ in range(ITERS) for _, rows in CHUNKS]
         + [

time: 66 us -> 63.6 us (0.964)
  Pallas kernels: 64.6 us -> 62.2 us
    pallas_call x1, Pallas kernels: 63 us -> 60.6 us  [on_device(): pl.pallas_call(kernel, out_shape=(jax.ShapeDtypeStruct((1, 2, ROWS, U), B...]
where the time goes in v3:
time: 63.6 us; the launch traced here: 63.5 us
  Pallas kernels  62.2 us (98%)
  between operations  1.29 us (2%)
    pallas_call x1, Pallas kernels, on_device(): pl.pallas_call(kernel, out_shape=(jax.ShapeDtypeStruct((1, 2, ROWS, U), B...  60.6 us
    pallas_call x1, Pallas kernels, on_device(): pl.pallas_call(hand_over, out_shape=(jax.ShapeDtypeStruct((1, 2, ROWS, U)...  1.61 us

profile of v3, /device:TPU:1, one launch (start us, length us, event | category | flops | bytes accessed | tf_op | source)
XLA Modules:
  0.0 63.5 jit_solution(15747101465241549444)
XLA Ops:
  1.3 60.6 %sweeps.1 = (bf16[1,2,112,384]{3,2,1,0:T(8,128)(2,1)}, bf16[7,8]{1,0:T(8,128)(2,1)}) custom-call(s32[1,1,6]{2,1,0:T(1,128)} %conn_src.1, s32[1,1]{1,0:T(1,128)S(6)} %copy.12.conn_count, s32[64]{0:T(128)} %tile_map.1, s32[1,2,4]{2,1,0:T(2,128)} %well_cells.1, f32[1,2,4]{2,1,0:T(2,128)} %well_gain.1, bf16[1,2,112,384]{3,2,1,0:T(8,128)(2,1)} %rhs_hbm.1, ...), custom_call_target="tpu_custom_call" | custom-call | tf_op jit(solution)/shard_map/sweeps/pallas_call | solution.py:288
  61.9 1.6 %hand_over.1 = (bf16[1,2,112,384]{3,2,1,0:T(8,128)(2,1)}, bf16[7,8]{1,0:T(8,128)(2,1)}) custom-call(bf16[1,2,112,384]{3,2,1,0:T(8,128)(2,1)} %get-tuple-element.4.adj, bf16[7,8]{1,0:T(8,128)(2,1)} %get-tuple-element.5.coef), custom_call_target="tpu_custom_call" | custom-call | tf_op jit(solution)/shard_map/hand_over/pallas_call | solution.py:334

commit v4 on v3

--- a/solution.py
+++ b/solution.py
@@ -66,6 +66,7 @@
         p_rs,
         s_ss,
         s_rs,
+        token,
     ) = rest[ITERS * len(CHUNKS) :]
     c, g = lax.axis_index("areal"), lax.axis_index("layer")
 
@@ -80,9 +81,9 @@
         one.start()
 
     barrier = pltpu.get_barrier_semaphore()
-    for k in range(1, COLUMNS):
-        pl.semaphore_signal(barrier, inc=1, device_id=(lax.rem(c + k, COLUMNS), g), device_id_type=MESH)
-    for k in range(1, GROUPS):
+    for k in (1, 2, -1, -2, 15, 16, 17):
+        pl.semaphore_signal(barrier, inc=1, device_id=(lax.rem(c + k + COLUMNS, COLUMNS), g), device_id_type=MESH)
+    for k in (1, GROUPS - 1):
         pl.semaphore_signal(barrier, inc=1, device_id=(c, lax.rem(g + k, GROUPS)), device_id_type=MESH)
 
     count = conn_count[0, 0]
@@ -104,8 +105,19 @@
     for i in range(ITERS):
         lam[i, 2] = jnp.zeros((ROWS, U), BF16)
 
-    pl.semaphore_wait(barrier, COLUMNS + GROUPS - 2)
-
+    pl.semaphore_wait(barrier, 9)
+
+    up, down = lax.rem(g + 1, GROUPS), lax.rem(g + GROUPS - 1, GROUPS)
+
+    def tell(n):
+        for side, to in ((0, up), (1, down)):
+            pl.semaphore_signal(token.at[n, side], inc=1, device_id=(c, to), device_id_type=MESH)
+
+    def hear(n):
+        for side in range(2):
+            pl.semaphore_wait(token.at[n, side], 1)
+
+    tell(0)
     asks = []
     for k in ORDER:
         one = pltpu.make_async_remote_copy(
@@ -114,8 +126,6 @@
         )
         one.start()
         asks.append(one)
-
-    up, down = lax.rem(g + 1, GROUPS), lax.rem(g + GROUPS - 1, GROUPS)
 
     def send_vertical(i, h):
         first, rows = CHUNKS[h]
@@ -184,6 +194,9 @@
     for i in range(ITERS):
         for h, (first, rows) in enumerate(CHUNKS):
             at = pl.ds(first, rows)
+            step = i * len(CHUNKS) + h
+            hear(step)
+            tell(step + 1)
             for one in flying[i, h]:
                 one.wait_recv()
             below = jnp.where(g > 0, recvz[i, 0, at], jnp.zeros((rows, U), BF16))
@@ -244,6 +257,7 @@
     packed = jnp.dot(spread, pick, preferred_element_type=F32)
     scat[...] = packed.reshape(GROUPS, 1, 128)
 
+    hear(ITERS * len(CHUNKS))
     scats = []
     for k in range(1, GROUPS):
         to = lax.rem(g + k, GROUPS)
@@ -324,6 +338,7 @@
             dma((COLUMNS,)),
             dma((GROUPS,)),
             dma((GROUPS,)),
+            pltpu.SemaphoreType.REGULAR((ITERS * nc + 1, 2)),
         ],
         compiler_params=pltpu.CompilerParams(
             collective_id=0, has_side_effects=True, vmem_limit_bytes=56 * 1024 * 1024

time: 63.6 us -> 61.7 us (0.970)
  Pallas kernels: 62.2 us -> 60.2 us
    pallas_call x1, Pallas kernels: 60.6 us -> 58.6 us  [on_device(): pl.pallas_call(kernel, out_shape=(jax.ShapeDtypeStruct((1, 2, ROWS, U), B...]
where the time goes in v4:
time: 61.7 us; the launch traced here: 61.5 us
  Pallas kernels  60.2 us (98%)
  between operations  1.29 us (2%)
    pallas_call x1, Pallas kernels, on_device(): pl.pallas_call(kernel, out_shape=(jax.ShapeDtypeStruct((1, 2, ROWS, U), B...  58.6 us
    pallas_call x1, Pallas kernels, on_device(): pl.pallas_call(hand_over, out_shape=(jax.ShapeDtypeStruct((1, 2, ROWS, U)...  1.61 us

profile of v4, /device:TPU:1, one launch (start us, length us, event | category | flops | bytes accessed | tf_op | source)
XLA Modules:
  0.0 61.5 jit_solution(15174414592769907083)
XLA Ops:
  1.3 58.6 %sweeps.1 = (bf16[1,2,112,384]{3,2,1,0:T(8,128)(2,1)}, bf16[7,8]{1,0:T(8,128)(2,1)}) custom-call(s32[1,1,6]{2,1,0:T(1,128)} %conn_src.1, s32[1,1]{1,0:T(1,128)S(6)} %copy.12.conn_count, s32[64]{0:T(128)} %tile_map.1, s32[1,2,4]{2,1,0:T(2,128)} %well_cells.1, f32[1,2,4]{2,1,0:T(2,128)} %well_gain.1, bf16[1,2,112,384]{3,2,1,0:T(8,128)(2,1)} %rhs_hbm.1, ...), custom_call_target="tpu_custom_call" | custom-call | tf_op jit(solution)/shard_map/sweeps/pallas_call | solution.py:302
  59.9 1.6 %hand_over.1 = (bf16[1,2,112,384]{3,2,1,0:T(8,128)(2,1)}, bf16[7,8]{1,0:T(8,128)(2,1)}) custom-call(bf16[1,2,112,384]{3,2,1,0:T(8,128)(2,1)} %get-tuple-element.4.adj, bf16[7,8]{1,0:T(8,128)(2,1)} %get-tuple-element.5.coef), custom_call_target="tpu_custom_call" | custom-call | tf_op jit(solution)/shard_map/hand_over/pallas_call | solution.py:349

commit v5 on v4

--- a/solution.py
+++ b/solution.py
@@ -26,8 +26,8 @@
     conn_src,
     conn_count,
     tile_map,
-    well_cells,
-    well_gain,
+    cells_hbm,
+    gain_hbm,
     rhs_hbm,
     areal_hbm,
     vert_hbm,
@@ -50,6 +50,8 @@
     scat_in,
     adj,
     slot_ref,
+    well_cells,
+    well_gain,
     *rest,
 ):
     recv = [[rest[i * len(CHUNKS) + h] for h in range(len(CHUNKS))] for i in range(ITERS)]
@@ -76,6 +78,8 @@
         pltpu.make_async_copy(areal_hbm.at[0], w, load_sem.at[2]),
         pltpu.make_async_copy(sens_hbm.at[0], sens, load_sem.at[3]),
         pltpu.make_async_copy(basis_hbm.at[0], basis, load_sem.at[4]),
+        pltpu.make_async_copy(cells_hbm, well_cells, load_sem.at[5]),
+        pltpu.make_async_copy(gain_hbm, well_gain, load_sem.at[6]),
     ]
     for one in loads:
         one.start()
@@ -305,7 +309,7 @@
             jax.ShapeDtypeStruct((1, 2, ROWS, U), BF16),
             jax.ShapeDtypeStruct((PER, MODES // COLUMNS), BF16),
         ),
-        in_specs=[smem] * 5 + [hbm] * 5,
+        in_specs=[smem] * 3 + [hbm] * 7,
         out_specs=(hbm, pl.BlockSpec(memory_space=pltpu.VMEM)),
         scratch_shapes=[
             pltpu.VMEM((ITERS, 3, ROWS, U), BF16),
@@ -323,10 +327,12 @@
             pltpu.VMEM((GROUPS, 1, 128), F32),
             pltpu.VMEM((2, ROWS, U), BF16),
             pltpu.SMEM((NS,), I32),
+            pltpu.SMEM((1, 2, WELLS), I32),
+            pltpu.SMEM((1, 2, WELLS), F32),
         ]
         + [pltpu.VMEM((NS, rows, U), BF16) for _ in range(ITERS) for _, rows in CHUNKS]
         + [
-            dma((5,)),
+            dma((7,)),
             dma,
             dma((NS,)),
             dma((NS,)),

time: 61.7 us -> 61.7 us (level)
  no operation moved by 1% of the time
where the time goes in v5:
time: 61.7 us; the launch traced here: 61.5 us
  Pallas kernels  60.2 us (98%)
  between operations  1.29 us (2%)
    pallas_call x1, Pallas kernels, on_device(): pl.pallas_call(kernel, out_shape=(jax.ShapeDtypeStruct((1, 2, ROWS, U), B...  58.6 us
    pallas_call x1, Pallas kernels, on_device(): pl.pallas_call(hand_over, out_shape=(jax.ShapeDtypeStruct((1, 2, ROWS, U)...  1.61 us

profile of v5, /device:TPU:1, one launch (start us, length us, event | category | flops | bytes accessed | tf_op | source)
XLA Modules:
  0.0 61.5 jit_solution(8378229726786014421)
XLA Ops:
  1.3 58.6 %sweeps.1 = (bf16[1,2,112,384]{3,2,1,0:T(8,128)(2,1)}, bf16[7,8]{1,0:T(8,128)(2,1)}) custom-call(s32[1,1,6]{2,1,0:T(1,128)} %conn_src.1, s32[1,1]{1,0:T(1,128)S(6)} %copy.12.conn_count, s32[64]{0:T(128)} %tile_map.1, s32[1,2,4]{2,1,0:T(2,128)} %cells_hbm.1, f32[1,2,4]{2,1,0:T(2,128)} %gain_hbm.1, bf16[1,2,112,384]{3,2,1,0:T(8,128)(2,1)} %rhs_hbm.1, ...), custom_call_target="tpu_custom_call" | custom-call | tf_op jit(solution)/shard_map/sweeps/pallas_call | solution.py:306
  59.9 1.6 %hand_over.1 = (bf16[1,2,112,384]{3,2,1,0:T(8,128)(2,1)}, bf16[7,8]{1,0:T(8,128)(2,1)}) custom-call(bf16[1,2,112,384]{3,2,1,0:T(8,128)(2,1)} %get-tuple-element.4.adj, bf16[7,8]{1,0:T(8,128)(2,1)} %get-tuple-element.5.coef), custom_call_target="tpu_custom_call" | custom-call | tf_op jit(solution)/shard_map/hand_over/pallas_call | solution.py:355
